TPU v7x, 128 devices: a whole 4x4x4 slice. The times are simulated.
128 devices in a mesh: src: 8 (over x, z_hi), tgt: 16 (over y, z_lo, core).
Axes of the slice: x: 4, y: 4, z: 4 (z_hi: 2, z_lo: 2; z = z_hi * 2 + z_lo), core: 2. Of those that a mesh axis runs over, the one named last changes fastest.
Arguments:
- noise: bfloat16 [4096, 2048], P(('src', 'tgt')), may hold values from -6 to 6
- data: bfloat16 [4096, 2048], P(('src', 'tgt')), may hold values from -6 to 6
- t_index: int32 [4096], P(('src', 'tgt')), may hold values from 0 to 1000
- embed_weight: bfloat16 [64, 2048], replicated, may hold values from -0.75 to 0.75
- position: bfloat16 [32, 2048], replicated, may hold values from -6 to 6
- norm_gain: float32 [2048], replicated, may hold values from 0.5 to 1.5
- qkv_weight: bfloat16 [2048, 6144], P(None, 'tgt'), may hold values from -0.125 to 0.125
Outputs:
- velocity: bfloat16 [4096, 2048], P(('src', 'tgt'))
- qkv: bfloat16 [131072, 6144], P(('src', 'tgt'))
All inputs are finite; a program needn't handle non-finite values.
Results may differ from a plain program's by a relative error of at most 0.014.
Values may be sent and summed in bfloat16 or wider, within the bound.
No kernel may reach another device: no remote copies, remote signals or barrier semaphores. Data moves between devices by JAX's collectives and lax.ppermute only.
A program may use at most 448 MiB of HBM per device.

v0:
```python
import jax
import jax.numpy as jnp
from jax import lax
from jax.sharding import PartitionSpec as P

ITERS = 3
TGRID = 1000


def shared(value, axis, count):
    spread = lax.optimization_barrier(jnp.broadcast_to(value[None], (count,) + value.shape))
    return lax.all_to_all(spread, axis, 0, 0)


def lse(scores, dim):
    peak = jnp.max(scores, axis=dim, keepdims=True)
    total = jnp.sum(jnp.exp(scores - peak), axis=dim)
    return jnp.squeeze(peak, dim) + jnp.log(total)


def halves(value):
    high = value.astype(jnp.bfloat16)
    low = (value - high.astype(jnp.float32)).astype(jnp.bfloat16)
    return (high, low)


def folded_weights(embed_weight, position, norm_gain, qkv_weight):
    scaled = jnp.concatenate([embed_weight, position], 0).astype(jnp.float32) * norm_gain
    high, low = halves(scaled)
    both = jnp.dot(jnp.concatenate([high, low], 0), qkv_weight, preferred_element_type=jnp.float32)
    rows = scaled.shape[0]
    return jnp.concatenate(halves(both[:rows] + both[rows:]), 0)


def local(noise, data, t_index, embed_weight, position, norm_gain, qkv_weight):
    latent = noise.shape[1]
    own = noise.shape[0]
    n_src = lax.axis_size("src")
    n_tgt = lax.axis_size("tgt")
    folded = lax.all_gather(
        folded_weights(embed_weight, position, norm_gain, qkv_weight), "tgt", axis=1, tiled=True
    )
    noise_block = lax.all_gather(noise, "tgt", axis=0, tiled=True)
    data_block = lax.all_gather(data, "src", axis=0, tiled=True)
    noise_sq = jnp.sum(jnp.square(noise_block.astype(jnp.float32)), axis=1)
    data_sq = jnp.sum(jnp.square(data_block.astype(jnp.float32)), axis=1)
    cross_term = lax.dot_general(
        noise_block, data_block, (((1,), (1,)), ((), ())), preferred_element_type=jnp.float32
    )
    cost = (noise_sq[:, None] + data_sq[None, :] - 2.0 * cross_term) / latent
    col_pot = jnp.zeros((data_block.shape[0],), jnp.float32)
    epsilon = 0.04
    for step in range(ITERS):
        epsilon = 0.04 * 0.45**step
        part = lse((col_pot[None, :] - cost) / epsilon, 1)
        row_pot = -epsilon * lse(shared(part, "tgt", n_tgt), 0)
        part = lse((row_pot[:, None] - cost) / epsilon, 0)
        col_pot = -epsilon * lse(shared(part, "src", n_src), 0)
    scores = (col_pot[None, :] - cost) / epsilon
    total = lse(shared(lse(scores, 1), "tgt", n_tgt), 0)
    coupling = jnp.exp(scores - total[:, None]).astype(jnp.bfloat16)
    partial_sum = jnp.dot(coupling, data_block, preferred_element_type=jnp.float32)
    pieces = lax.all_to_all(
        partial_sum.astype(jnp.bfloat16).reshape(n_tgt, own, latent), "tgt", 0, 0
    )
    target = jnp.sum(pieces.astype(jnp.float32), axis=0)
    noise_own = noise.astype(jnp.float32)
    velocity = (target - noise_own).astype(jnp.bfloat16)
    times = t_index.astype(jnp.float32) / TGRID
    mixed = ((1.0 - times)[:, None] * noise_own + times[:, None] * target).astype(jnp.bfloat16)
    patch_in, width = embed_weight.shape
    patch_count = position.shape[0]
    patches = mixed.reshape(own * patch_count, patch_in)
    embedded = jnp.dot(patches, embed_weight, preferred_element_type=jnp.float32)
    embedded = embedded.reshape(own, patch_count, width) + position.astype(jnp.float32)[None]
    scale = lax.rsqrt(jnp.mean(embedded * embedded, axis=-1) + 1e-06).reshape(own * patch_count)
    place = jnp.tile(jnp.eye(patch_count, dtype=jnp.bfloat16), (own, 1))
    tokens = jnp.concatenate([patches, place, patches, place], 1)
    qkv = jnp.dot(tokens, folded, preferred_element_type=jnp.float32) * scale[:, None]
    return (velocity, qkv.astype(jnp.bfloat16))


def solution(mesh):
    return jax.shard_map(
        local,
        mesh=mesh,
        in_specs=(
            P(("src", "tgt"), None),
            P(("src", "tgt"), None),
            P(("src", "tgt")),
            P(),
            P(),
            P(),
            P(None, "tgt"),
        ),
        out_specs=(P(("src", "tgt"), None), P(("src", "tgt"), None)),
        check_vma=False,
    )
```

profile of v0, /device:TPU:33, one launch (start us, length us, event | category | flops | bytes accessed | tf_op | source)
XLA Modules:
  0.0 236.3 jit_solution(10667740617140354199)
XLA Ops:
  7.2 0.7 all-gather.6.cloned.1.call-update
  8.0 0.7 all-gather.4.cloned.1.call-update
  8.7 49.3 %all-gather.6.cloned.1.call-done = bf16[256,2048]{1,0:T(8,128)(2,1)} async-done(((bf16[32,2048]{1,0:T(8,128)(2,1)}), bf16[256,2048]{1,0:T(8,128)(2,1)}) %all-gather.6.cloned.1.call-update) | async-done | bytes 1048592 | tf_op jit(solution)/shard_map/all_gather | solution.py:44
  58.0 1.6 multiply_reduce_fusion.2
  59.6 34.7 %all-gather.4.cloned.1.call-done = bf16[512,2048]{1,0:T(8,128)(2,1)} async-done(((bf16[32,2048]{1,0:T(8,128)(2,1)}), bf16[512,2048]{1,0:T(8,128)(2,1)}) %all-gather.4.cloned.1.call-update) | async-done | bytes 2097168 | tf_op jit(solution)/shard_map/all_gather | solution.py:43
  94.3 2.2 multiply_reduce_fusion.1
  96.6 0.9 fusion.14
  97.7 9.3 %all_to_all.89 = f32[16,1,512]{2,1,0:T(1,128)S(1)} all-to-all(f32[16,1,512]{2,1,0:T(1,128)S(1)} %all_to_all.59), channel_id=1, replica_groups=mesh['src'=8,'tgt'=16] {'tgt'}, dimensions={0} | all-to-all | bytes 65536 | tf_op jit(solution)/shard_map/all_to_all | solution.py:12
  107.5 11.8 %all_to_all.90 = f32[8,1,256]{2,1,0:T(1,128)S(1)} all-to-all(f32[8,1,256]{2,1,0:T(1,128)S(1)} %all_to_all.62), channel_id=1, replica_groups=mesh['src'=8,'tgt'=16] {'src'}, dimensions={0} | all-to-all | bytes 16384 | tf_op jit(solution)/shard_map/all_to_all | solution.py:12
  119.7 0.6 all_to_all.65
  120.4 6.8 %all-to-all-start.2 = ((f32[16,1,512]{2,1,0:T(1,128)}), f32[16,1,512]{2,1,0:T(1,128)S(1)}, u32[]{:S(2)}, u32[]{:S(2)}) async-start(f32[16,1,512]{2,1,0:T(1,128)} %all_to_all.65), calls=%async_computation.2 | async-start | bytes 65536 | tf_op jit(solution)/shard_map/all_to_all | solution.py:12
  127.2 2.0 fusion.6
  129.1 2.8 %all-to-all-done.2 = f32[16,1,512]{2,1,0:T(1,128)S(1)} async-done(((f32[16,1,512]{2,1,0:T(1,128)}), f32[16,1,512]{2,1,0:T(1,128)S(1)}, u32[]{:S(2)}, u32[]{:S(2)}) %all-to-all-start.2) | async-done | bytes 32800 | tf_op jit(solution)/shard_map/all_to_all | solution.py:12
  133.0 3.3 %all-to-all-start.3 = ((f32[8,1,256]{2,1,0:T(1,128)}), f32[8,1,256]{2,1,0:T(1,128)S(1)}, u32[]{:S(2)}, u32[]{:S(2)}) async-start(f32[8,1,256]{2,1,0:T(1,128)} %all_to_all.68), calls=%async_computation.3 | async-start | bytes 16384 | tf_op jit(solution)/shard_map/all_to_all | solution.py:12
  136.4 2.4 %fusion.2 = f32[192,384]{1,0:T(8,128)} fusion(bf16[2048,384]{1,0:T(8,128)(2,1)S(1)} %copy-done, bf16[96,2048]{1,0:T(8,128)(2,1)} %get-tuple-element.5, bf16[96,2048]{1,0:T(8,128)(2,1)} %get-tuple-element.4), kind=kOutput, calls=%fused_computation.9 | convolution fusion | flops 303562752 | bytes 2654208 | tf_op jit(solution)/shard_map/dot_general | solution.py:30
  138.8 4.0 %all-to-all-done.3 = f32[8,1,256]{2,1,0:T(1,128)S(1)} async-done(((f32[8,1,256]{2,1,0:T(1,128)}), f32[8,1,256]{2,1,0:T(1,128)S(1)}, u32[]{:S(2)}, u32[]{:S(2)}) %all-to-all-start.3) | async-done | bytes 8224 | tf_op jit(solution)/shard_map/all_to_all | solution.py:12
  143.2 0.6 all_to_all.71
  143.9 5.9 %all-to-all-start.4 = ((f32[16,1,512]{2,1,0:T(1,128)}), f32[16,1,512]{2,1,0:T(1,128)S(1)}, u32[]{:S(2)}, u32[]{:S(2)}) async-start(f32[16,1,512]{2,1,0:T(1,128)} %all_to_all.71), calls=%async_computation.4 | async-start | bytes 65536 | tf_op jit(solution)/shard_map/all_to_all | solution.py:12
  149.8 1.0 subtract_convert_fusion.1
  150.8 3.8 %all-to-all-done.4 = f32[16,1,512]{2,1,0:T(1,128)S(1)} async-done(((f32[16,1,512]{2,1,0:T(1,128)}), f32[16,1,512]{2,1,0:T(1,128)S(1)}, u32[]{:S(2)}, u32[]{:S(2)}) %all-to-all-start.4) | async-done | bytes 32800 | tf_op jit(solution)/shard_map/all_to_all | solution.py:12
  155.1 0.6 all_to_all.74
  155.7 3.3 %all-to-all-start.5 = ((f32[8,1,256]{2,1,0:T(1,128)}), f32[8,1,256]{2,1,0:T(1,128)S(1)}, u32[]{:S(2)}, u32[]{:S(2)}) async-start(f32[8,1,256]{2,1,0:T(1,128)} %all_to_all.74), calls=%async_computation.5 | async-start | bytes 16384 | tf_op jit(solution)/shard_map/all_to_all | solution.py:12
  159.1 0.7 pad_maximum_fusion.1
  159.8 5.7 %all-to-all-done.5 = f32[8,1,256]{2,1,0:T(1,128)S(1)} async-done(((f32[8,1,256]{2,1,0:T(1,128)}), f32[8,1,256]{2,1,0:T(1,128)S(1)}, u32[]{:S(2)}, u32[]{:S(2)}) %all-to-all-start.5) | async-done | bytes 8224 | tf_op jit(solution)/shard_map/all_to_all | solution.py:12
  165.9 9.8 %all_to_all.91 = f32[16,1,512]{2,1,0:T(1,128)S(1)} all-to-all(f32[16,1,512]{2,1,0:T(1,128)S(1)} %all_to_all.77), channel_id=1, replica_groups=mesh['src'=8,'tgt'=16] {'tgt'}, dimensions={0} | all-to-all | bytes 65536 | tf_op jit(solution)/shard_map/all_to_all | solution.py:12
  175.8 2.2 convolution_convert_fusion
  178.0 5.8 %all-to-all-start.7 = ((bf16[16,32,2048]{2,1,0:T(8,128)(2,1)}), bf16[16,32,2048]{2,1,0:T(8,128)(2,1)}, u32[]{:S(2)}, u32[]{:S(2)}) async-start(bf16[16,32,2048]{2,1,0:T(8,128)(2,1)} %bitcast.53), calls=%async_computation.7 | async-start | bytes 4194304 | tf_op jit(solution)/shard_map/all_to_all | solution.py:63
  183.9 32.7 %all-to-all-done.7 = bf16[16,32,2048]{2,1,0:T(8,128)(2,1)} async-done(((bf16[16,32,2048]{2,1,0:T(8,128)(2,1)}), bf16[16,32,2048]{2,1,0:T(8,128)(2,1)}, u32[]{:S(2)}, u32[]{:S(2)}) %all-to-all-start.7) | async-done | bytes 2097184 | tf_op jit(solution)/shard_map/all_to_all | solution.py:63
  216.6 2.0 convert_reduce_fusion
  218.6 0.7 fusion.23
  219.8 1.3 multiply_reduce_fusion
  221.3 8.5 %multiply_convert_fusion = bf16[1024,6144]{1,0:T(8,128)(2,1)} fusion(f32[1024]{0:T(1024)S(1)} %rsqrt.11, bf16[192,6144]{1,0:T(8,128)(2,1)} %all-gather.8.cloned.1.call-done, bf16[1024,32]{1,0:T(8,128)(2,1)S(1)} %bitcast.54, bf16[1024,64]{1,0:T(8,128)(2,1)S(1)} %reshape.161), kind=kOutput, calls=%fused_computation | convolution fusion | flops 2430074880 | bytes 15142912 | tf_op jit(solution)/shard_map/dot_general | solution.py:79
  (81 shorter events, 4.3 us)
Async XLA Ops:
  7.2 129.2 %copy-start = (bf16[2048,384]{1,0:T(8,128)(2,1)S(1)}, bf16[2048,384]{1,0:T(8,128)(2,1)}, u32[]{:S(2)}) copy-start(bf16[2048,384]{1,0:T(8,128)(2,1)} %param.13) | copy-start | bytes 4718596
  7.2 50.8 %all-gather.6.cloned.1.call-start = ((), (), s32[]{:S(2)}) async-start(), calls=%async_computation.9 | async-start | bytes 1179648 | tf_op jit(solution)/shard_map/all_gather | solution.py:44
  7.9 86.4 %all-gather.4.cloned.1.call-start = ((), (), s32[]{:S(2)}) async-start(), calls=%async_computation.8 | async-start | bytes 2228224 | tf_op jit(solution)/shard_map/all_gather | solution.py:43
  58.0 38.6 %copy-start.1 = (bf16[256,2048]{1,0:T(8,128)(2,1)S(1)}, bf16[256,2048]{1,0:T(8,128)(2,1)}, u32[]{:S(2)}) copy-start(bf16[256,2048]{1,0:T(8,128)(2,1)} %all-gather.6.cloned.1.call-done) | copy-start | bytes 3145732
  94.3 2.2 copy-start.2
  97.5 29.6 %copy-start.3 = (bf16[32,2048]{1,0:T(8,128)(2,1)S(1)}, bf16[32,2048]{1,0:T(8,128)(2,1)}, u32[]{:S(2)}) copy-start(bf16[32,2048]{1,0:T(8,128)(2,1)} %param.11) | copy-start | bytes 393220
  97.5 29.6 %copy-start.6 = (f32[2048]{0:T(1024)S(1)}, f32[2048]{0:T(1024)}, u32[]{:S(2)}) copy-start(f32[2048]{0:T(1024)} %param.12) | copy-start | bytes 24580
  120.4 11.6 %all-to-all-start.2 = ((f32[16,1,512]{2,1,0:T(1,128)}), f32[16,1,512]{2,1,0:T(1,128)S(1)}, u32[]{:S(2)}, u32[]{:S(2)}) async-start(f32[16,1,512]{2,1,0:T(1,128)} %all_to_all.65), calls=%async_computation.2 | async-start | bytes 65536 | tf_op jit(solution)/shard_map/all_to_all | solution.py:12
  133.0 9.8 %all-to-all-start.3 = ((f32[8,1,256]{2,1,0:T(1,128)}), f32[8,1,256]{2,1,0:T(1,128)S(1)}, u32[]{:S(2)}, u32[]{:S(2)}) async-start(f32[8,1,256]{2,1,0:T(1,128)} %all_to_all.68), calls=%async_computation.3 | async-start | bytes 16384 | tf_op jit(solution)/shard_map/all_to_all | solution.py:12
  143.9 10.7 %all-to-all-start.4 = ((f32[16,1,512]{2,1,0:T(1,128)}), f32[16,1,512]{2,1,0:T(1,128)S(1)}, u32[]{:S(2)}, u32[]{:S(2)}) async-start(f32[16,1,512]{2,1,0:T(1,128)} %all_to_all.71), calls=%async_computation.4 | async-start | bytes 65536 | tf_op jit(solution)/shard_map/all_to_all | solution.py:12
  155.7 9.8 %all-to-all-start.5 = ((f32[8,1,256]{2,1,0:T(1,128)}), f32[8,1,256]{2,1,0:T(1,128)S(1)}, u32[]{:S(2)}, u32[]{:S(2)}) async-start(f32[8,1,256]{2,1,0:T(1,128)} %all_to_all.74), calls=%async_computation.5 | async-start | bytes 16384 | tf_op jit(solution)/shard_map/all_to_all | solution.py:12
  159.0 62.2 %all-gather.8.cloned.1.call-start = ((), (), s32[]{:S(2)}) async-start(), calls=%async_computation.10 | async-start | bytes 2506752 | tf_op jit(solution)/shard_map/all_gather | solution.py:40
  178.0 5.8 %copy-start.7 = (s32[32]{0:T(128)S(1)}, s32[32]{0:T(128)}, u32[]{:S(2)}) copy-start(s32[32]{0:T(128)} %param.9) | copy-start | bytes 388
  178.0 38.6 %all-to-all-start.7 = ((bf16[16,32,2048]{2,1,0:T(8,128)(2,1)}), bf16[16,32,2048]{2,1,0:T(8,128)(2,1)}, u32[]{:S(2)}, u32[]{:S(2)}) async-start(bf16[16,32,2048]{2,1,0:T(8,128)(2,1)} %bitcast.53), calls=%async_computation.7 | async-start | bytes 4194304 | tf_op jit(solution)/shard_map/all_to_all | solution.py:63
  183.8 34.8 %copy-start.4 = (bf16[32,2048]{1,0:T(8,128)(2,1)S(1)}, bf16[32,2048]{1,0:T(8,128)(2,1)}, u32[]{:S(2)}) copy-start(bf16[32,2048]{1,0:T(8,128)(2,1)} %param.7) | copy-start | bytes 393220
  183.8 36.0 %copy-start.5 = (bf16[64,2048]{1,0:T(8,128)(2,1)S(1)}, bf16[64,2048]{1,0:T(8,128)(2,1)}, u32[]{:S(2)}) copy-start(bf16[64,2048]{1,0:T(8,128)(2,1)} %param.10) | copy-start | bytes 786436
Sparse Core Ops, SparseCore 0:
  10.4 47.5 all-gather.5
  59.7 34.5 all-gather.3
  161.5 46.7 all-gather.7
where the time goes:
time: 237 us; the launch traced here: 236 us
  waiting for transfers between devices  135 us (57%)
  blocking collectives  30.9 us (13%)
  starting transfers between devices  25.2 us (11%)
  matrix products  15.3 us (6%)
  between operations  14.1 us (6%)
  other arithmetic  13 us (5%)
  local copies, waits for them, and re-layouts  3.21 us (1%)
    all_gather x1, waiting for transfers between devices, local(): data_block = lax.all_gather(data, 'src', axis=0, tiled=True)  49.3 us
    all_gather x1, waiting for transfers between devices, local(): noise_block = lax.all_gather(noise, 'tgt', axis=0, tiled=True)  34.7 us
    all_to_all x1, waiting for transfers between devices, local(): lax.all_to_all(partial_sum.astype(jnp.bfloat16).reshape(n_tgt, own, laten...  32.7 us
    all_to_all x3, blocking collectives, shared(): return lax.all_to_all(spread, axis, 0, 0)  30.9 us
    all_to_all x4, starting transfers between devices, shared(): return lax.all_to_all(spread, axis, 0, 0)  19.4 us
    all_to_all x4, waiting for transfers between devices, shared(): return lax.all_to_all(spread, axis, 0, 0)  16.4 us
    dot_general x1, matrix products, local(): jnp.dot(tokens, folded, preferred_element_type=jnp.float32) * scale[:, None]  8.46 us
    all_to_all x1, starting transfers between devices, local(): lax.all_to_all(partial_sum.astype(jnp.bfloat16).reshape(n_tgt, own, laten...  5.76 us
  transfers between devices with their start and end apart: 8, of which 7 were waited for; matrix products, arithmetic and copies ran while one was open for 6% of the time, Pallas kernels for 0%

commit v1 on v0

--- a/solution.py
+++ b/solution.py
@@ -5,6 +5,11 @@
 
 ITERS = 3
 TGRID = 1000
+
+
+def gather_over(shard, axis, d):
+    outgoing = jnp.stack([shard] * lax.axis_size(axis))
+    return jnp.concatenate(lax.all_to_all(outgoing, axis, 0, 0), axis=d)
 
 
 def shared(value, axis, count):
@@ -40,7 +45,7 @@
     folded = lax.all_gather(
         folded_weights(embed_weight, position, norm_gain, qkv_weight), "tgt", axis=1, tiled=True
     )
-    noise_block = lax.all_gather(noise, "tgt", axis=0, tiled=True)
+    noise_block = gather_over(noise, "tgt", 0)
     data_block = lax.all_gather(data, "src", axis=0, tiled=True)
     noise_sq = jnp.sum(jnp.square(noise_block.astype(jnp.float32)), axis=1)
     data_sq = jnp.sum(jnp.square(data_block.astype(jnp.float32)), axis=1)

time: 237 us -> 217 us (0.916)
  waiting for transfers between devices: 135 us -> 102 us
  starting transfers between devices: 25.2 us -> 31.5 us
  local copies, waits for them, and re-layouts: 3.21 us -> 5.77 us
    all_gather x1 -> x0, waiting for transfers between devices: 34.7 us -> none  [local(): noise_block = lax.all_gather(noise, 'tgt', axis=0, tiled=True)]
    all_to_all x0 -> x1, starting transfers between devices: none -> 6.26 us  [gather_over(): return jnp.concatenate(lax.all_to_all(outgoing, axis, 0, 0), axis=d)]
    another operation x0 -> x1, local copies, waits for them, and re-layouts: none -> 2.48 us  [gather_over(): outgoing = jnp.stack([shard] * lax.axis_size(axis))]
    all_gather x1, waiting for transfers between devices: 49.3 us -> 51.8 us  [local(): data_block = lax.all_gather(data, 'src', axis=0, tiled=True)]
  transfers between devices with their start and end apart: 8 -> 8, of which waited for: 7 -> 6; matrix products, arithmetic and copies ran while one was open for 6% -> 8% of each run, Pallas kernels for 0% -> 0%
where the time goes in v1:
time: 217 us; the launch traced here: 216 us
  waiting for transfers between devices  102 us (47%)
  blocking collectives  31.9 us (15%)
  starting transfers between devices  31.5 us (15%)
  matrix products  16.8 us (8%)
  between operations  15.8 us (7%)
  other arithmetic  12.8 us (6%)
  local copies, waits for them, and re-layouts  5.77 us (3%)
    all_gather x1, waiting for transfers between devices, local(): data_block = lax.all_gather(data, 'src', axis=0, tiled=True)  51.8 us
    all_to_all x1, waiting for transfers between devices, local(): lax.all_to_all(partial_sum.astype(jnp.bfloat16).reshape(n_tgt, own, laten...  33.2 us
    all_to_all x3, blocking collectives, shared(): return lax.all_to_all(spread, axis, 0, 0)  31.9 us
    all_to_all x4, starting transfers between devices, shared(): return lax.all_to_all(spread, axis, 0, 0)  19.4 us
    all_to_all x4, waiting for transfers between devices, shared(): return lax.all_to_all(spread, axis, 0, 0)  16.4 us
    dot_general x1, matrix products, local(): jnp.dot(tokens, folded, preferred_element_type=jnp.float32) * scale[:, None]  8.46 us
    all_to_all x1, starting transfers between devices, gather_over(): return jnp.concatenate(lax.all_to_all(outgoing, axis, 0, 0), axis=d)  6.26 us
    all_to_all x1, starting transfers between devices, local(): lax.all_to_all(partial_sum.astype(jnp.bfloat16).reshape(n_tgt, own, laten...  5.77 us
  transfers between devices with their start and end apart: 8, of which 6 were waited for; matrix products, arithmetic and copies ran while one was open for 8% of the time, Pallas kernels for 0%

profile of v1, /device:TPU:33, one launch (start us, length us, event | category | flops | bytes accessed | tf_op | source)
XLA Modules:
  0.0 216.5 jit_solution(6961906513983472249)
XLA Ops:
  8.1 0.7 all-gather.3.cloned.1.call-update
  8.7 2.5 %stack.2 = bf16[16,32,2048]{2,1,0:T(8,128)(2,1)} broadcast(bf16[32,2048]{1,0:T(8,128)(2,1)} %param.7), dimensions={1,2} | broadcast | bytes 2228224 | tf_op jit(solution)/shard_map/stack | solution.py:11
  11.2 6.3 %all-to-all-start = ((bf16[16,32,2048]{2,1,0:T(8,128)(2,1)}), bf16[16,32,2048]{2,1,0:T(8,128)(2,1)}, u32[]{:S(2)}, u32[]{:S(2)}) async-start(bf16[16,32,2048]{2,1,0:T(8,128)(2,1)} %stack.2), calls=%async_computation | async-start | bytes 4194304 | tf_op jit(solution)/shard_map/all_to_all | solution.py:12
  17.5 51.8 %all-gather.3.cloned.1.call-done = bf16[256,2048]{1,0:T(8,128)(2,1)} async-done(((bf16[32,2048]{1,0:T(8,128)(2,1)}), bf16[256,2048]{1,0:T(8,128)(2,1)}) %all-gather.3.cloned.1.call-update) | async-done | bytes 1048592 | tf_op jit(solution)/shard_map/all_gather | solution.py:49
  69.3 1.6 multiply_reduce_fusion.2
  70.9 2.1 multiply_reduce_fusion.1
  73.0 2.4 %fusion.14 = (f32[512]{0:T(512)S(1)}, f32[512,256]{0,1:T(8,128)S(1)}) fusion(bf16[512,2048]{1,0:T(8,128)(2,1)} %bitcast, bf16[256,2048]{1,0:T(8,128)(2,1)S(1)} %copy-done.1, f32[256]{0:T(256)S(1)} %multiply_reduce_fusion.2, f32[512]{0:T(512)S(1)} %add.138), kind=kOutput, calls=%fused_computation.38 | convolution fusion | flops 537787904 | bytes 3675136 | tf_op jit(solution)/shard_map/dot_general | solution.py:52
  75.6 11.5 %all_to_all.94 = f32[16,1,512]{2,1,0:T(1,128)S(1)} all-to-all(f32[16,1,512]{2,1,0:T(1,128)S(1)} %all_to_all.63), channel_id=1, replica_groups=mesh['src'=8,'tgt'=16] {'tgt'}, dimensions={0} | all-to-all | bytes 65536 | tf_op jit(solution)/shard_map/all_to_all | solution.py:17
  87.7 10.5 %all_to_all.95 = f32[8,1,256]{2,1,0:T(1,128)S(1)} all-to-all(f32[8,1,256]{2,1,0:T(1,128)S(1)} %all_to_all.66), channel_id=1, replica_groups=mesh['src'=8,'tgt'=16] {'src'}, dimensions={0} | all-to-all | bytes 16384 | tf_op jit(solution)/shard_map/all_to_all | solution.py:17
  98.6 0.6 all_to_all.69
  99.2 6.8 %all-to-all-start.3 = ((f32[16,1,512]{2,1,0:T(1,128)}), f32[16,1,512]{2,1,0:T(1,128)S(1)}, u32[]{:S(2)}, u32[]{:S(2)}) async-start(f32[16,1,512]{2,1,0:T(1,128)} %all_to_all.69), calls=%async_computation.3 | async-start | bytes 65536 | tf_op jit(solution)/shard_map/all_to_all | solution.py:17
  106.0 2.0 fusion.6
  108.0 2.8 %all-to-all-done.3 = f32[16,1,512]{2,1,0:T(1,128)S(1)} async-done(((f32[16,1,512]{2,1,0:T(1,128)}), f32[16,1,512]{2,1,0:T(1,128)S(1)}, u32[]{:S(2)}, u32[]{:S(2)}) %all-to-all-start.3) | async-done | bytes 32800 | tf_op jit(solution)/shard_map/all_to_all | solution.py:17
  111.9 3.3 %all-to-all-start.4 = ((f32[8,1,256]{2,1,0:T(1,128)}), f32[8,1,256]{2,1,0:T(1,128)S(1)}, u32[]{:S(2)}, u32[]{:S(2)}) async-start(f32[8,1,256]{2,1,0:T(1,128)} %all_to_all.72), calls=%async_computation.4 | async-start | bytes 16384 | tf_op jit(solution)/shard_map/all_to_all | solution.py:17
  115.2 2.4 %fusion.2 = f32[192,384]{1,0:T(8,128)} fusion(bf16[2048,384]{1,0:T(8,128)(2,1)S(1)} %copy-done, bf16[96,2048]{1,0:T(8,128)(2,1)} %get-tuple-element.5, bf16[96,2048]{1,0:T(8,128)(2,1)} %get-tuple-element.4), kind=kOutput, calls=%fused_computation.9 | convolution fusion | flops 303562752 | bytes 2654208 | tf_op jit(solution)/shard_map/dot_general | solution.py:35
  117.6 4.0 %all-to-all-done.4 = f32[8,1,256]{2,1,0:T(1,128)S(1)} async-done(((f32[8,1,256]{2,1,0:T(1,128)}), f32[8,1,256]{2,1,0:T(1,128)S(1)}, u32[]{:S(2)}, u32[]{:S(2)}) %all-to-all-start.4) | async-done | bytes 8224 | tf_op jit(solution)/shard_map/all_to_all | solution.py:17
  122.1 0.6 all_to_all.75
  122.7 5.9 %all-to-all-start.5 = ((f32[16,1,512]{2,1,0:T(1,128)}), f32[16,1,512]{2,1,0:T(1,128)S(1)}, u32[]{:S(2)}, u32[]{:S(2)}) async-start(f32[16,1,512]{2,1,0:T(1,128)} %all_to_all.75), calls=%async_computation.5 | async-start | bytes 65536 | tf_op jit(solution)/shard_map/all_to_all | solution.py:17
  128.7 1.0 subtract_convert_fusion.1
  129.7 3.8 %all-to-all-done.5 = f32[16,1,512]{2,1,0:T(1,128)S(1)} async-done(((f32[16,1,512]{2,1,0:T(1,128)}), f32[16,1,512]{2,1,0:T(1,128)S(1)}, u32[]{:S(2)}, u32[]{:S(2)}) %all-to-all-start.5) | async-done | bytes 32800 | tf_op jit(solution)/shard_map/all_to_all | solution.py:17
  133.9 0.6 all_to_all.78
  134.5 3.3 %all-to-all-start.6 = ((f32[8,1,256]{2,1,0:T(1,128)}), f32[8,1,256]{2,1,0:T(1,128)S(1)}, u32[]{:S(2)}, u32[]{:S(2)}) async-start(f32[8,1,256]{2,1,0:T(1,128)} %all_to_all.78), calls=%async_computation.6 | async-start | bytes 16384 | tf_op jit(solution)/shard_map/all_to_all | solution.py:17
  137.9 0.7 pad_maximum_fusion.1
  138.6 5.7 %all-to-all-done.6 = f32[8,1,256]{2,1,0:T(1,128)S(1)} async-done(((f32[8,1,256]{2,1,0:T(1,128)}), f32[8,1,256]{2,1,0:T(1,128)S(1)}, u32[]{:S(2)}, u32[]{:S(2)}) %all-to-all-start.6) | async-done | bytes 8224 | tf_op jit(solution)/shard_map/all_to_all | solution.py:17
  144.8 9.8 %all_to_all.96 = f32[16,1,512]{2,1,0:T(1,128)S(1)} all-to-all(f32[16,1,512]{2,1,0:T(1,128)S(1)} %all_to_all.81), channel_id=1, replica_groups=mesh['src'=8,'tgt'=16] {'tgt'}, dimensions={0} | all-to-all | bytes 65536 | tf_op jit(solution)/shard_map/all_to_all | solution.py:17
  154.7 2.2 %convolution_convert_fusion = bf16[512,2048]{1,0:T(8,128)(2,1)} fusion(bf16[256,2048]{1,0:T(8,128)(2,1)S(1)} %copy-done.1, f32[512,256]{0,1:T(8,128)S(1)} %get-tuple-element.11, f32[512]{0:T(512)S(1)} %log_add_fusion, f32[256]{0:T(256)S(1)} %add_multiply_fusion.3), kind=kOutput, calls=%fused_computation.4 | convolution fusion | flops 538443776 | bytes 3673088 | tf_op jit(solution)/shard_map/dot_general | solution.py:67
  156.9 5.8 %all-to-all-start.8 = ((bf16[16,32,2048]{2,1,0:T(8,128)(2,1)}), bf16[16,32,2048]{2,1,0:T(8,128)(2,1)}, u32[]{:S(2)}, u32[]{:S(2)}) async-start(bf16[16,32,2048]{2,1,0:T(8,128)(2,1)} %bitcast.54), calls=%async_computation.8 | async-start | bytes 4194304 | tf_op jit(solution)/shard_map/all_to_all | solution.py:68
  162.7 33.2 %all-to-all-done.8 = bf16[16,32,2048]{2,1,0:T(8,128)(2,1)} async-done(((bf16[16,32,2048]{2,1,0:T(8,128)(2,1)}), bf16[16,32,2048]{2,1,0:T(8,128)(2,1)}, u32[]{:S(2)}, u32[]{:S(2)}) %all-to-all-start.8) | async-done | bytes 2097184 | tf_op jit(solution)/shard_map/all_to_all | solution.py:68
  195.9 2.0 convert_reduce_fusion
  197.9 0.7 fusion.23
  199.1 1.3 multiply_reduce_fusion
  200.6 8.5 %multiply_convert_fusion = bf16[1024,6144]{1,0:T(8,128)(2,1)} fusion(f32[1024]{0:T(1024)S(1)} %rsqrt.11, bf16[192,6144]{1,0:T(8,128)(2,1)} %all-gather.5.cloned.1.call-done, bf16[1024,32]{1,0:T(8,128)(2,1)S(1)} %bitcast.55, bf16[1024,64]{1,0:T(8,128)(2,1)S(1)} %reshape.169), kind=kOutput, calls=%fused_computation | convolution fusion | flops 2430074880 | bytes 15142912 | tf_op jit(solution)/shard_map/dot_general | solution.py:84
  (80 shorter events, 4.3 us)
Async XLA Ops:
  8.0 107.2 %copy-start = (bf16[2048,384]{1,0:T(8,128)(2,1)S(1)}, bf16[2048,384]{1,0:T(8,128)(2,1)}, u32[]{:S(2)}) copy-start(bf16[2048,384]{1,0:T(8,128)(2,1)} %param.13) | copy-start | bytes 4718596
  8.0 61.2 %all-gather.3.cloned.1.call-start = ((), (), s32[]{:S(2)}) async-start(), calls=%async_computation.9 | async-start | bytes 1179648 | tf_op jit(solution)/shard_map/all_gather | solution.py:49
  11.2 59.6 %all-to-all-start = ((bf16[16,32,2048]{2,1,0:T(8,128)(2,1)}), bf16[16,32,2048]{2,1,0:T(8,128)(2,1)}, u32[]{:S(2)}, u32[]{:S(2)}) async-start(bf16[16,32,2048]{2,1,0:T(8,128)(2,1)} %stack.2), calls=%async_computation | async-start | bytes 4194304 | tf_op jit(solution)/shard_map/all_to_all | solution.py:12
  69.3 3.8 %copy-start.1 = (bf16[256,2048]{1,0:T(8,128)(2,1)S(1)}, bf16[256,2048]{1,0:T(8,128)(2,1)}, u32[]{:S(2)}) copy-start(bf16[256,2048]{1,0:T(8,128)(2,1)} %all-gather.3.cloned.1.call-done) | copy-start | bytes 3145732
  75.4 30.6 %copy-start.2 = (bf16[32,2048]{1,0:T(8,128)(2,1)S(1)}, bf16[32,2048]{1,0:T(8,128)(2,1)}, u32[]{:S(2)}) copy-start(bf16[32,2048]{1,0:T(8,128)(2,1)} %param.11) | copy-start | bytes 393220
  75.4 30.6 %copy-start.5 = (f32[2048]{0:T(1024)S(1)}, f32[2048]{0:T(1024)}, u32[]{:S(2)}) copy-start(f32[2048]{0:T(1024)} %param.12) | copy-start | bytes 24580
  99.2 11.6 %all-to-all-start.3 = ((f32[16,1,512]{2,1,0:T(1,128)}), f32[16,1,512]{2,1,0:T(1,128)S(1)}, u32[]{:S(2)}, u32[]{:S(2)}) async-start(f32[16,1,512]{2,1,0:T(1,128)} %all_to_all.69), calls=%async_computation.3 | async-start | bytes 65536 | tf_op jit(solution)/shard_map/all_to_all | solution.py:17
  111.9 9.8 %all-to-all-start.4 = ((f32[8,1,256]{2,1,0:T(1,128)}), f32[8,1,256]{2,1,0:T(1,128)S(1)}, u32[]{:S(2)}, u32[]{:S(2)}) async-start(f32[8,1,256]{2,1,0:T(1,128)} %all_to_all.72), calls=%async_computation.4 | async-start | bytes 16384 | tf_op jit(solution)/shard_map/all_to_all | solution.py:17
  122.7 10.7 %all-to-all-start.5 = ((f32[16,1,512]{2,1,0:T(1,128)}), f32[16,1,512]{2,1,0:T(1,128)S(1)}, u32[]{:S(2)}, u32[]{:S(2)}) async-start(f32[16,1,512]{2,1,0:T(1,128)} %all_to_all.75), calls=%async_computation.5 | async-start | bytes 65536 | tf_op jit(solution)/shard_map/all_to_all | solution.py:17
  134.5 9.8 %all-to-all-start.6 = ((f32[8,1,256]{2,1,0:T(1,128)}), f32[8,1,256]{2,1,0:T(1,128)S(1)}, u32[]{:S(2)}, u32[]{:S(2)}) async-start(f32[8,1,256]{2,1,0:T(1,128)} %all_to_all.78), calls=%async_computation.6 | async-start | bytes 16384 | tf_op jit(solution)/shard_map/all_to_all | solution.py:17
  137.9 62.7 %all-gather.5.cloned.1.call-start = ((), (), s32[]{:S(2)}) async-start(), calls=%async_computation.10 | async-start | bytes 2506752 | tf_op jit(solution)/shard_map/all_gather | solution.py:45
  156.9 5.8 %copy-start.6 = (s32[32]{0:T(128)S(1)}, s32[32]{0:T(128)}, u32[]{:S(2)}) copy-start(s32[32]{0:T(128)} %param.9) | copy-start | bytes 388
  156.9 39.0 %all-to-all-start.8 = ((bf16[16,32,2048]{2,1,0:T(8,128)(2,1)}), bf16[16,32,2048]{2,1,0:T(8,128)(2,1)}, u32[]{:S(2)}, u32[]{:S(2)}) async-start(bf16[16,32,2048]{2,1,0:T(8,128)(2,1)} %bitcast.54), calls=%async_computation.8 | async-start | bytes 4194304 | tf_op jit(solution)/shard_map/all_to_all | solution.py:68
  162.7 35.3 %copy-start.3 = (bf16[32,2048]{1,0:T(8,128)(2,1)S(1)}, bf16[32,2048]{1,0:T(8,128)(2,1)}, u32[]{:S(2)}) copy-start(bf16[32,2048]{1,0:T(8,128)(2,1)} %param.7) | copy-start | bytes 393220
  162.7 36.5 %copy-start.4 = (bf16[64,2048]{1,0:T(8,128)(2,1)S(1)}, bf16[64,2048]{1,0:T(8,128)(2,1)}, u32[]{:S(2)}) copy-start(bf16[64,2048]{1,0:T(8,128)(2,1)} %param.10) | copy-start | bytes 786436
Sparse Core Ops, SparseCore 0:
  11.2 58.0 all-gather.2
Sparse Core Ops, SparseCore 1:
  140.0 46.7 all-gather.4
